TPU v7x, 32 devices: a whole 2x2x4 slice. The times are simulated.
32 devices in a mesh: ctx: 8 (over z, y), tp: 4 (over x, core).
Axes of the slice: x: 2, y: 2, z: 4, core: 2. Of those that a mesh axis runs over, the one named last changes fastest.
Arguments:
- short_query: bfloat16 [1024, 2048], P('ctx', 'tp'), may hold values from -6 to 6
- short_key: bfloat16 [1024, 2048], P('ctx', 'tp'), may hold values from -6 to 6
- short_value: bfloat16 [1024, 2048], P('ctx', 'tp'), may hold values from -6 to 6
- short_filter: bfloat16 [128, 2048], P(None, 'tp'), may hold values from -0.5 to 0.5
- long_query: bfloat16 [1024, 2048], P('ctx', 'tp'), may hold values from -6 to 6
- long_key: bfloat16 [1024, 2048], P('ctx', 'tp'), may hold values from -6 to 6
- long_filter: bfloat16 [1024, 2048], P('ctx', 'tp'), may hold values from -0.1875 to 0.1875
- out_weight: bfloat16 [2048, 2048], P('tp'), may hold values from -0.125 to 0.125
- out_grad: bfloat16 [1024, 2048], P('ctx', 'tp'), may hold values from -6 to 6
Outputs:
- short_query_grad: bfloat16 [1024, 2048], P('ctx', 'tp')
- short_key_grad: bfloat16 [1024, 2048], P('ctx', 'tp')
- short_value_grad: bfloat16 [1024, 2048], P('ctx', 'tp')
- short_filter_grad: bfloat16 [128, 2048], P(None, 'tp')
- long_query_grad: bfloat16 [1024, 2048], P('ctx', 'tp')
- long_key_grad: bfloat16 [1024, 2048], P('ctx', 'tp')
- long_filter_grad: bfloat16 [1024, 2048], P('ctx', 'tp')
All inputs are finite; a program needn't handle non-finite values.
Results may differ from a plain program's by a relative error of at most 0.015.
Values may be sent and summed in bfloat16 or wider, within the bound.
A program may use at most 64 MiB of HBM per device.

v0:
```python
import functools
import math

import jax
import jax.numpy as jnp
import ml_dtypes
import numpy as np
from jax import lax
from jax.experimental import pallas as pl
from jax.experimental.pallas import tpu as pltpu
from jax.sharding import PartitionSpec as P

MESH = pl.DeviceIdType.MESH
BF16 = jnp.bfloat16
F32 = jnp.float32
LONGEST_DENSE = 2048
VMEM_GRANT = 60 * 1024 * 1024
PARTS = ("prod", "gates", "grad", "smix", "lmix", "filt", "back", "bone")


def passed_along(block, axis, distance):
    devices = range(lax.axis_size(axis))
    route = [(i - distance, i) for i in devices if i - distance in devices]
    return lax.ppermute(block, axis, route)


def angle_tables(blocks, inner):
    size_one = 2 * blocks
    whole = size_one * inner
    first = (
        lax.broadcasted_iota(jnp.int32, (size_one, blocks), 0)
        * lax.broadcasted_iota(jnp.int32, (size_one, blocks), 1)
        % size_one
    )
    phase_one = first.astype(jnp.float32) * (2.0 * math.pi / size_one)
    twist = (
        lax.broadcasted_iota(jnp.int32, (size_one, inner), 0)
        * lax.broadcasted_iota(jnp.int32, (size_one, inner), 1)
        % whole
    )
    phase_twist = twist.astype(jnp.float32) * (2.0 * math.pi / whole)
    second = (
        lax.broadcasted_iota(jnp.int32, (inner, inner), 0)
        * lax.broadcasted_iota(jnp.int32, (inner, inner), 1)
        % inner
    )
    phase_two = second.astype(jnp.float32) * (2.0 * math.pi / inner)
    return (
        jnp.cos(phase_one),
        jnp.sin(phase_one),
        jnp.cos(phase_twist)[:, None, :],
        jnp.sin(phase_twist)[:, None, :],
        jnp.cos(phase_two),
        jnp.sin(phase_two),
        whole,
    )


def spectrum(values, tables):
    cos_one, sin_one, cos_twist, sin_twist, cos_two, sin_two, whole = tables
    highest = lax.Precision.HIGHEST
    real_a = jnp.einsum("kn,ncm->kcm", cos_one, values, precision=highest)
    imag_a = -jnp.einsum("kn,ncm->kcm", sin_one, values, precision=highest)
    real_b = real_a * cos_twist + imag_a * sin_twist
    imag_b = imag_a * cos_twist - real_a * sin_twist
    real_c = jnp.einsum("kcm,mq->kcq", real_b, cos_two, precision=highest) + jnp.einsum(
        "kcm,mq->kcq", imag_b, sin_two, precision=highest
    )
    imag_c = jnp.einsum("kcm,mq->kcq", imag_b, cos_two, precision=highest) - jnp.einsum(
        "kcm,mq->kcq", real_b, sin_two, precision=highest
    )
    return (real_c, imag_c)


def restore(real_in, imag_in, tables, both):
    cos_one, sin_one, cos_twist, sin_twist, cos_two, sin_two, whole = tables
    highest = lax.Precision.HIGHEST
    real_p = jnp.einsum("kcq,qm->kcm", real_in, cos_two, precision=highest) - jnp.einsum(
        "kcq,qm->kcm", imag_in, sin_two, precision=highest
    )
    imag_p = jnp.einsum("kcq,qm->kcm", imag_in, cos_two, precision=highest) + jnp.einsum(
        "kcq,qm->kcm", real_in, sin_two, precision=highest
    )
    real_q = real_p * cos_twist - imag_p * sin_twist
    imag_q = imag_p * cos_twist + real_p * sin_twist
    real_out = (
        jnp.einsum("kn,kcm->ncm", cos_one, real_q, precision=highest)
        - jnp.einsum("kn,kcm->ncm", sin_one, imag_q, precision=highest)
    ) / whole
    if both:
        imag_out = (
            jnp.einsum("kn,kcm->ncm", cos_one, imag_q, precision=highest)
            + jnp.einsum("kn,kcm->ncm", sin_one, real_q, precision=highest)
        ) / whole
        return (real_out, imag_out)
    return real_out


def spectral(product, gated, filter_in):
    blocks, count, inner = product.shape
    tables = angle_tables(blocks, inner)
    real_u, imag_u = spectrum(product.astype(jnp.float32), tables)
    real_g, imag_g = spectrum(gated.astype(jnp.float32), tables)
    real_h, imag_h = spectrum(filter_in.astype(jnp.float32), tables)
    real_pair = real_h * real_u - imag_h * imag_u - real_h * imag_g + imag_h * real_g
    imag_pair = real_h * imag_u + imag_h * real_u + real_h * real_g + imag_h * imag_g
    conv_part, back_part = restore(real_pair, imag_pair, tables, True)
    filter_part = restore(
        real_u * real_g + imag_u * imag_g, real_u * imag_g - imag_u * real_g, tables, False
    )
    return (conv_part, back_part, filter_part)


def tap_sum(extended, weights, token_rows, causal):
    filter_taps, channels = weights.shape

    def group_step(group, total):
        for inner in range(8):
            place = group * 8 + inner
            weight_row = lax.dynamic_index_in_dim(weights, place, 0, keepdims=False).astype(
                jnp.float32
            )
            start = filter_taps - 1 - place if causal else place
            shifted = lax.dynamic_slice_in_dim(extended, start, token_rows, 0).astype(jnp.float32)
            total = total + weight_row[None, :] * shifted
        return total

    return lax.fori_loop(
        0, filter_taps // 8, group_step, jnp.zeros((token_rows, channels), jnp.float32)
    )


def filter_terms(extended, grads, filter_taps):
    token_rows, channels = grads.shape

    def group_terms(group):
        partials = []
        for inner in range(8):
            place = group * 8 + inner
            shifted = lax.dynamic_slice_in_dim(
                extended, filter_taps - 1 - place, token_rows, 0
            ).astype(jnp.float32)
            partials.append(jnp.sum(grads * shifted, axis=0))
        return jnp.stack(partials)

    stacked = lax.map(group_terms, jnp.arange(filter_taps // 8, dtype=jnp.int32))
    return stacked.reshape(filter_taps, channels)


def general_body(
    short_query,
    short_key,
    short_value,
    short_filter,
    long_query,
    long_key,
    long_filter,
    out_weight,
    out_grad,
):
    token_rows, channels = short_query.shape
    groups = lax.axis_size("ctx")
    seq_len = token_rows * groups
    scaling = 1.0 / math.sqrt(seq_len)
    filter_taps = short_filter.shape[0]
    product_one = (short_key.astype(jnp.float32) * short_value.astype(jnp.float32)).astype(
        jnp.bfloat16
    )
    before = passed_along(product_one[token_rows - (filter_taps - 1) :], "ctx", 1)
    extended_prod = jnp.concatenate([before, product_one], axis=0)
    short_mix = tap_sum(extended_prod, short_filter, token_rows, True)
    mixed = (short_query.astype(jnp.float32) * short_mix).astype(jnp.bfloat16)
    grad_two = lax.dot_general(
        lax.all_gather(out_grad, "tp", axis=1, tiled=True),
        out_weight,
        (((1,), (1,)), ((), ())),
        preferred_element_type=jnp.float32,
    ).astype(jnp.bfloat16)

    def to_channels(values):
        return values.T.reshape(groups, channels // groups, token_rows)

    def to_tokens(values):
        return values.reshape(channels, token_rows).T

    product_two = (long_key.astype(jnp.float32) * mixed.astype(jnp.float32)).astype(jnp.bfloat16)
    gated_two = (grad_two.astype(jnp.float32) * long_query.astype(jnp.float32)).astype(jnp.bfloat16)
    conv_part, back_part, filter_part = spectral(
        lax.all_to_all(to_channels(product_two), "ctx", split_axis=0, concat_axis=0, tiled=True),
        lax.all_to_all(to_channels(gated_two), "ctx", split_axis=0, concat_axis=0, tiled=True),
        lax.all_to_all(to_channels(long_filter), "ctx", split_axis=0, concat_axis=0, tiled=True),
    )
    long_mix = lax.all_to_all(conv_part, "ctx", split_axis=0, concat_axis=0, tiled=True)
    back_two = lax.all_to_all(back_part, "ctx", split_axis=0, concat_axis=0, tiled=True)
    filter_two = lax.all_to_all(filter_part, "ctx", split_axis=0, concat_axis=0, tiled=True)
    long_mix = to_tokens(long_mix)
    back_two = to_tokens(back_two)
    filter_two = to_tokens(filter_two)
    long_query_grad = (grad_two.astype(jnp.float32) * long_mix).astype(jnp.bfloat16)
    long_key_grad = (back_two * mixed.astype(jnp.float32)).astype(jnp.bfloat16)
    mixed_grad = (back_two * long_key.astype(jnp.float32)).astype(jnp.bfloat16)
    long_filter_grad = (filter_two * scaling).astype(jnp.bfloat16)
    gated_one = (mixed_grad.astype(jnp.float32) * short_query.astype(jnp.float32)).astype(
        jnp.bfloat16
    )
    short_query_grad = (mixed_grad.astype(jnp.float32) * short_mix).astype(jnp.bfloat16)
    after = passed_along(gated_one[: filter_taps - 1], "ctx", -1)
    extended_grad = jnp.concatenate([gated_one, after], axis=0)
    back_one = tap_sum(extended_grad, short_filter, token_rows, False)
    short_key_grad = (back_one * short_value.astype(jnp.float32)).astype(jnp.bfloat16)
    short_value_grad = (back_one * short_key.astype(jnp.float32)).astype(jnp.bfloat16)
    local_terms = filter_terms(extended_prod, gated_one.astype(jnp.float32), filter_taps)
    filter_one = lax.psum(local_terms, "ctx")
    short_filter_grad = (filter_one * scaling).astype(jnp.bfloat16)
    return (
        short_query_grad,
        short_key_grad,
        short_value_grad,
        short_filter_grad,
        long_query_grad,
        long_key_grad,
        long_filter_grad,
    )


def wave_tables(seq_len):
    time = np.arange(seq_len, dtype=np.int64)[:, None]
    odd = 2 * np.arange(seq_len, dtype=np.int64)[None, :] + 1
    phase = (time * odd % (4 * seq_len)).astype(np.float64) * (math.pi / (2 * seq_len))
    forward = np.concatenate([np.cos(phase), np.sin(phase)], axis=1)
    return (
        forward.astype(ml_dtypes.bfloat16),
        np.ascontiguousarray(forward.T).astype(ml_dtypes.bfloat16),
    )


def dot(a, b):
    return jnp.dot(a, b, preferred_element_type=F32)


def flipped(block):
    return block.astype(F32).T.astype(BF16)


def operator_kernel(
    n, m,
    sq_in, sk_in, sv_in, sf_in, lq_in, lk_in, lf_in, og_in, weight, forward, inverse,
    sq_grad, lq_grad, lk_grad, lf_grad, bone_out, taps_out,
    smix_rx, lmix_rx, filt_rx, back_rx, taps_rx, results, sq, sk, sv, lk, sf, lq, lf, og, grad, weight_v, fwd, inv, og_rx, tx_prod, tx_gates, tx_grad, rx_prod, rx_gates, rx_grad,
    tx_smix, tx_lmix, tx_filt, tx_back, tx_bone, tx_taps, filter_t, signals, smix,
    spec_prod, spec_sf, spec_u, spec_h, waves, load_sem, own_sem, og_send, og_recv, taps_send, taps_recv,
    send, recv,
):
    me = lax.axis_index("ctx")
    col = lax.axis_index("tp")
    rows, chans = sq.shape
    cb = chans // n
    taps = sf.shape[0]
    seq = rows * n
    tile = 2 * rows
    kt = 256

    barrier = pltpu.get_barrier_semaphore()
    for d in range(1, n):
        pl.semaphore_signal(
            barrier, inc=1, device_id=(lax.rem(me + d, n), col), device_id_type=MESH
        )
    for d in range(1, m):
        pl.semaphore_signal(
            barrier, inc=1, device_id=(me, lax.rem(col + d, m)), device_id_type=MESH
        )

    loads = {}
    for place, (name, source, target) in enumerate((
        ("sk", sk_in, sk), ("sv", sv_in, sv), ("og", og_in, og), ("lf", lf_in, lf),
        ("lk", lk_in, lk), ("sq", sq_in, sq), ("sf", sf_in, sf), ("fwd", forward, fwd),
        ("lq", lq_in, lq), ("weight", weight, weight_v), ("inv", inverse, inv),
    )):
        loads[name] = pltpu.make_async_copy(source, target, load_sem.at[place])
        loads[name].start()

    loads["sk"].wait()
    loads["sv"].wait()
    tx_prod[...] = (sk[...].astype(F32) * sv[...].astype(F32)).T.astype(BF16)
    loads["og"].wait()
    pl.semaphore_wait(barrier, n + m - 2)

    og_copies = []
    for d in range(1, m):
        copy = pltpu.make_async_remote_copy(
            src_ref=og,
            dst_ref=og_rx.at[d - 1],
            send_sem=og_send.at[d - 1],
            recv_sem=og_recv.at[d - 1],
            device_id=(me, lax.rem(col + d, m)),
            device_id_type=MESH,
        )
        copy.start()
        og_copies.append(copy)

    own_rows = pl.ds(pl.multiple_of(me * cb, cb), cb)
    sent = {}

    def exchange(part, source, target):
        place = PARTS.index(part)
        copies = []
        for d in range(1, n):
            peer = lax.rem(me + d, n)
            copy = pltpu.make_async_remote_copy(
                src_ref=source(peer),
                dst_ref=target,
                send_sem=send.at[place, d - 1],
                recv_sem=recv.at[place, d - 1],
                device_id=(peer, col),
                device_id_type=MESH,
            )
            copy.start()
            copies.append(copy)
        sent[part] = copies

    kept = []

    def keep(source, target):
        copy = pltpu.make_async_copy(source, target, own_sem.at[len(kept)])
        copy.start()
        kept.append(copy)

    def arrived(part):
        for copy in sent[part]:
            copy.wait_recv()

    def row_block(peer):
        return pl.ds(pl.multiple_of(peer * cb, cb), cb)

    exchange("prod", lambda peer: tx_prod.at[row_block(peer)], rx_prod.at[me])
    rx_prod[me] = tx_prod[own_rows]
    loads["lf"].wait()
    tx_gates[0] = flipped(lf[...])
    loads["lk"].wait()
    loads["sq"].wait()
    tx_gates[1] = (lk[...].astype(F32) * sq[...].astype(F32)).T.astype(BF16)
    exchange("gates", lambda peer: tx_gates.at[:, row_block(peer)], rx_gates.at[me])
    for place in range(2):
        rx_gates[me, place] = tx_gates[place, own_rows]
    loads["sf"].wait()
    filter_t[...] = flipped(sf[...])

    def tiles(k):
        start = pl.multiple_of(k * kt, kt)
        return pl.ds(start, kt), pl.ds(pl.multiple_of(seq + start, kt), kt)

    def halves(rows_in, depth, k):
        cos_at, sin_at = tiles(k)
        return dot(rows_in, fwd[:depth, cos_at]), dot(rows_in, fwd[:depth, sin_at])

    arrived("prod")
    for s in range(n):
        signals[0:cb, s * rows : (s + 1) * rows] = rx_prod[s]
    loads["fwd"].wait()

    def short_step(k, carry):
        cos_at, sin_at = tiles(k)
        pc, ps = halves(signals[0:cb, :], seq, k)
        fc, fs = halves(filter_t[own_rows, :], taps, k)
        spec_prod[:, cos_at] = pc
        spec_prod[:, sin_at] = ps
        spec_sf[:, cos_at] = fc
        spec_sf[:, sin_at] = fs
        waves[0:cb, cos_at] = (pc * fc - ps * fs).astype(BF16)
        waves[0:cb, sin_at] = (pc * fs + ps * fc).astype(BF16)
        return carry

    lax.fori_loop(0, seq // kt, short_step, 0)
    loads["inv"].wait()

    def at_tokens(step):
        return pl.ds(pl.multiple_of(step * tile, tile), tile)

    def put(target, step, values):
        for b in range(2):
            target[step * 2 + b] = values[:, b * rows : (b + 1) * rows].astype(BF16)

    def short_back(step, carry):
        mix = dot(waves[0:cb, :], inv[:, at_tokens(step)]) * (1.0 / seq)
        smix[:, at_tokens(step)] = mix
        put(tx_smix, step, mix)
        return carry

    lax.fori_loop(0, n // 2, short_back, 0)

    loads["weight"].wait()
    loads["lq"].wait()
    total = jnp.zeros((chans, rows), F32)
    for d in range(m):
        if d > 0:
            og_copies[d - 1].wait_recv()
        owner = lax.rem(col + m - d, m)
        features = pl.ds(pl.multiple_of(owner * chans, chans), chans)
        block = og[...] if d == 0 else og_rx[d - 1]
        total = total + lax.dot_general(
            weight_v[:, features], block, (((1,), (1,)), ((), ())), preferred_element_type=F32
        )
    grad[...] = total.astype(BF16)
    tx_grad[...] = (grad[...].astype(F32) * lq[...].astype(F32).T).astype(BF16)
    exchange("grad", lambda peer: tx_grad.at[row_block(peer)], rx_grad.at[me])
    rx_grad[me] = tx_grad[own_rows]
    exchange("smix", lambda peer: tx_smix.at[peer], smix_rx.at[own_rows])
    smix_rx[own_rows, :] = tx_smix[me]

    arrived("gates")
    for s in range(n):
        at = slice(s * rows, (s + 1) * rows)
        signals[0:cb, at] = (rx_gates[s, 1].astype(F32) * smix[:, at]).astype(BF16)
        signals[cb : 2 * cb, at] = rx_gates[s, 0]

    def long_step(k, carry):
        cos_at, sin_at = tiles(k)
        c, s = halves(signals[0 : 2 * cb, :], seq, k)
        spec_u[:, cos_at] = c[0:cb]
        spec_u[:, sin_at] = s[0:cb]
        spec_h[:, cos_at] = c[cb:]
        spec_h[:, sin_at] = s[cb:]
        waves[0:cb, cos_at] = (c[0:cb] * c[cb:] - s[0:cb] * s[cb:]).astype(BF16)
        waves[0:cb, sin_at] = (c[0:cb] * s[cb:] + s[0:cb] * c[cb:]).astype(BF16)
        return carry

    lax.fori_loop(0, seq // kt, long_step, 0)

    def mix_back(step, carry):
        put(tx_lmix, step, dot(waves[0:cb, :], inv[:, at_tokens(step)]) * (1.0 / seq))
        return carry

    lax.fori_loop(0, n // 2, mix_back, 0)
    exchange("lmix", lambda peer: tx_lmix.at[peer], lmix_rx.at[own_rows])
    lmix_rx[own_rows, :] = tx_lmix[me]

    arrived("grad")
    for s in range(n):
        signals[2 * cb : 3 * cb, s * rows : (s + 1) * rows] = rx_grad[s]

    def grad_step(k, carry):
        cos_at, sin_at = tiles(k)
        c, s = halves(signals[2 * cb : 3 * cb, :], seq, k)
        uc, us = spec_u[:, cos_at], spec_u[:, sin_at]
        hc, hs = spec_h[:, cos_at], spec_h[:, sin_at]
        waves[cb : 2 * cb, cos_at] = (hc * c + hs * s).astype(BF16)
        waves[cb : 2 * cb, sin_at] = (hc * s - hs * c).astype(BF16)
        waves[2 * cb : 3 * cb, cos_at] = (uc * c + us * s).astype(BF16)
        waves[2 * cb : 3 * cb, sin_at] = (uc * s - us * c).astype(BF16)
        return carry

    lax.fori_loop(0, seq // kt, grad_step, 0)

    def long_back(step, carry):
        mixes = dot(waves[cb:, :], inv[:, at_tokens(step)]) * (1.0 / seq)
        put(tx_back, step, mixes[0:cb])
        put(tx_filt, step, mixes[cb:] * (1.0 / math.sqrt(seq)))
        smix[:, at_tokens(step)] = mixes[0:cb]
        return carry

    lax.fori_loop(0, n // 2, long_back, 0)
    for part, source, target in (
        ("back", tx_back, back_rx), ("filt", tx_filt, filt_rx)
    ):
        exchange(part, lambda peer, source=source: source.at[peer], target.at[own_rows])
        target[own_rows, :] = source[me]

    for s in range(n):
        at = slice(s * rows, (s + 1) * rows)
        signals[0:cb, at] = (smix[:, at] * rx_gates[s, 1].astype(F32)).astype(BF16)

    def gate_step(k, carry):
        cos_at, sin_at = tiles(k)
        c, s = halves(signals[0:cb, :], seq, k)
        pc, ps = spec_prod[:, cos_at], spec_prod[:, sin_at]
        fc, fs = spec_sf[:, cos_at], spec_sf[:, sin_at]
        waves[0:cb, cos_at] = (fc * c + fs * s).astype(BF16)
        waves[0:cb, sin_at] = (fc * s - fs * c).astype(BF16)
        waves[cb : 2 * cb, cos_at] = (pc * c + ps * s).astype(BF16)
        waves[cb : 2 * cb, sin_at] = (pc * s - ps * c).astype(BF16)
        return carry

    lax.fori_loop(0, seq // kt, gate_step, 0)

    terms = dot(waves[cb : 2 * cb, :], inv[:, 0:taps]) * (1.0 / (seq * math.sqrt(seq)))
    tx_taps[...] = terms.astype(BF16)
    taps_rx[own_rows, :] = tx_taps[...]
    pair = me + 1 - 2 * lax.rem(me, 2)

    def taps_copy(place, source, target_rows, peer):
        copy = pltpu.make_async_remote_copy(
            src_ref=source,
            dst_ref=taps_rx.at[target_rows],
            send_sem=taps_send.at[place],
            recv_sem=taps_recv.at[place],
            device_id=(peer, col),
            device_id_type=MESH,
        )
        copy.start()
        return copy

    far = [
        taps_copy(d - 1, tx_taps, own_rows, lax.rem(me + 2 * d, n)) for d in range(1, n // 2)
    ]
    near = [taps_copy(n // 2 - 1, tx_taps, own_rows, pair)]

    def short_grad(step, carry):
        put(tx_bone, step, dot(waves[0:cb, :], inv[:, at_tokens(step)]) * (1.0 / seq))
        return carry

    lax.fori_loop(0, n // 2, short_grad, 0)
    exchange("bone", lambda peer: tx_bone.at[peer], bone_out.at[own_rows])
    keep(tx_bone.at[me], bone_out.at[own_rows])

    def finish(place, target, values):
        results[place] = values.T.astype(BF16)
        keep(results.at[place], target)

    arrived("smix")
    arrived("lmix")
    finish(0, lq_grad, grad[...].astype(F32) * lmix_rx[...].astype(F32))
    arrived("back")
    back = back_rx[...].astype(F32).T
    mix = smix_rx[...].astype(F32).T
    mixed = (sq[...].astype(F32) * mix).astype(BF16).astype(F32)
    results[1] = (back * mixed).astype(BF16)
    keep(results.at[1], lk_grad)
    mixed_grad = (back * lk[...].astype(F32)).astype(BF16).astype(F32)
    results[2] = (mixed_grad * mix).astype(BF16)
    keep(results.at[2], sq_grad)
    arrived("filt")
    finish(3, lf_grad, filt_rx[...].astype(F32))

    for d in range(1, n // 2):
        far[d - 1].wait_recv()
        source = row_block(lax.rem(me + n - 2 * d, n))
        near.append(taps_copy(n // 2 - 1 + d, taps_rx.at[source], source, pair))
    for copy in near:
        copy.wait_recv()
    keep(taps_rx, taps_out)

    arrived("bone")
    for part in PARTS:
        for copy in sent[part]:
            copy.wait_send()
    for copy in og_copies + far + near:
        copy.wait_send()
    for copy in kept:
        copy.wait()


def finish_kernel(
    sq_done, lq_done, lk_done, lf_done, bone, taps, sk, sv,
    sq_grad, sk_grad, sv_grad, sf_grad, lq_grad, lk_grad, lf_grad,
    bone_v, taps_v, sk_v, sv_v, sk_out, sv_out, sf_out, move_sem,
):
    def move(place, source, target):
        copy = pltpu.make_async_copy(source, target, move_sem.at[place])
        copy.start()
        return copy

    loads = [
        move(place, source, target)
        for place, (source, target) in enumerate(
            ((bone, bone_v), (sv, sv_v), (sk, sk_v), (taps, taps_v))
        )
    ]
    moves = [
        move(4 + place, source, target)
        for place, (source, target) in enumerate(
            ((sq_done, sq_grad), (lq_done, lq_grad), (lk_done, lk_grad), (lf_done, lf_grad))
        )
    ]
    loads[0].wait()
    back_one = bone_v[...].astype(F32).T
    loads[1].wait()
    sk_out[...] = (back_one * sv_v[...].astype(F32)).astype(BF16)
    moves.append(move(8, sk_out, sk_grad))
    loads[2].wait()
    sv_out[...] = (back_one * sk_v[...].astype(F32)).astype(BF16)
    moves.append(move(9, sv_out, sv_grad))
    loads[3].wait()
    sf_out[...] = flipped(taps_v[...])
    moves.append(move(10, sf_out, sf_grad))
    for copy in moves:
        copy.wait()


def dense_body(
    n, m, sq, sk, sv, sf, lq, lk, lf, weight, og
):
    rows, chans = sq.shape
    taps = sf.shape[0]
    seq = rows * n
    cb = chans // n
    forward, inverse = wave_tables(seq)
    hbm = pl.BlockSpec(memory_space=pltpu.HBM)
    tokens = jax.ShapeDtypeStruct((rows, chans), BF16)
    turned = jax.ShapeDtypeStruct((chans, rows), BF16)
    blocks = pltpu.VMEM((n, cb, rows), BF16)
    spectrum = pltpu.VMEM((cb, 2 * seq), F32)
    sent_on = pl.pallas_call(
        functools.partial(operator_kernel, n, m),
        out_shape=[tokens] * 4 + [turned, jax.ShapeDtypeStruct((chans, taps), BF16)],
        in_specs=[hbm] * 11,
        out_specs=[hbm] * 6,
        scratch_shapes=[
            pltpu.VMEM((chans, rows), BF16),
            pltpu.VMEM((chans, rows), BF16),
            pltpu.VMEM((chans, rows), BF16),
            pltpu.VMEM((chans, rows), BF16),
            pltpu.VMEM((chans, taps), BF16),
            pltpu.VMEM((4, rows, chans), BF16),
            pltpu.VMEM((rows, chans), BF16),
            pltpu.VMEM((rows, chans), BF16),
            pltpu.VMEM((rows, chans), BF16),
            pltpu.VMEM((rows, chans), BF16),
            pltpu.VMEM((taps, chans), BF16),
            pltpu.VMEM((rows, chans), BF16),
            pltpu.VMEM((rows, chans), BF16),
            pltpu.VMEM((rows, chans), BF16),
            pltpu.VMEM((chans, rows), BF16),
            pltpu.VMEM(weight.shape, BF16),
            pltpu.VMEM(forward.shape, BF16),
            pltpu.VMEM(inverse.shape, BF16),
            pltpu.VMEM((m - 1, rows, chans), BF16),
            pltpu.VMEM((chans, rows), BF16),
            pltpu.VMEM((2, chans, rows), BF16),
            pltpu.VMEM((chans, rows), BF16),
            blocks,
            pltpu.VMEM((n, 2, cb, rows), BF16),
            blocks,
            blocks, blocks, blocks, blocks, blocks,
            pltpu.VMEM((cb, taps), BF16),
            pltpu.VMEM((chans, taps), BF16),
            pltpu.VMEM((3 * cb, seq), BF16),
            pltpu.VMEM((cb, seq), F32),
            spectrum, spectrum, spectrum, spectrum,
            pltpu.VMEM((3 * cb, 2 * seq), BF16),
            pltpu.SemaphoreType.DMA((11,)),
            pltpu.SemaphoreType.DMA((6,)),
            pltpu.SemaphoreType.DMA((m - 1,)),
            pltpu.SemaphoreType.DMA((m - 1,)),
            pltpu.SemaphoreType.DMA((n - 1,)),
            pltpu.SemaphoreType.DMA((n - 1,)),
            pltpu.SemaphoreType.DMA((len(PARTS), n - 1)),
            pltpu.SemaphoreType.DMA((len(PARTS), n - 1)),
        ],
        compiler_params=pltpu.CompilerParams(
            collective_id=0, has_side_effects=True, vmem_limit_bytes=VMEM_GRANT
        ),
    )(sq, sk, sv, sf, lq, lk, lf, og, weight, jnp.asarray(forward), jnp.asarray(inverse))
    short = jax.ShapeDtypeStruct((taps, chans), BF16)
    return pl.pallas_call(
        finish_kernel,
        out_shape=[tokens] * 3 + [short] + [tokens] * 3,
        in_specs=[hbm] * 8,
        out_specs=[hbm] * 7,
        scratch_shapes=[
            pltpu.VMEM((chans, rows), BF16),
            pltpu.VMEM((chans, taps), BF16),
            pltpu.VMEM((rows, chans), BF16),
            pltpu.VMEM((rows, chans), BF16),
            pltpu.VMEM((rows, chans), BF16),
            pltpu.VMEM((rows, chans), BF16),
            pltpu.VMEM((taps, chans), BF16),
            pltpu.SemaphoreType.DMA((11,)),
        ],
        compiler_params=pltpu.CompilerParams(vmem_limit_bytes=VMEM_GRANT),
    )(*sent_on, sk, sv)


def body(n, m, *arrays):
    rows, chans = arrays[0].shape
    taps = arrays[3].shape[0]
    dense = (
        rows * n <= LONGEST_DENSE
        and rows % 128 == 0
        and taps % 128 == 0
        and taps <= rows * n
        and n > 1
        and n % 2 == 0
        and m > 1
        and chans % (16 * n) == 0
        and chans % 128 == 0
    )
    if dense:
        return tuple(dense_body(n, m, *arrays))
    return general_body(*arrays)


def solution(mesh):
    in_specs = (
        P("ctx", "tp"),
        P("ctx", "tp"),
        P("ctx", "tp"),
        P(None, "tp"),
        P("ctx", "tp"),
        P("ctx", "tp"),
        P("ctx", "tp"),
        P("tp", None),
        P("ctx", "tp"),
    )
    out_specs = (
        P("ctx", "tp"),
        P("ctx", "tp"),
        P("ctx", "tp"),
        P(None, "tp"),
        P("ctx", "tp"),
        P("ctx", "tp"),
        P("ctx", "tp"),
    )
    return jax.shard_map(
        functools.partial(body, mesh.shape["ctx"], mesh.shape["tp"]), mesh=mesh, in_specs=in_specs, out_specs=out_specs, check_vma=False)
```

profile of v0, /device:TPU:0, one launch (start us, length us, event | category | flops | bytes accessed | tf_op | source)
XLA Modules:
  0.0 56.1 jit_solution(17487459756610258352)
XLA Ops:
  0.6 38.3 %shard_map.162 = (bf16[128,512]{1,0:T(8,128)(2,1)}, bf16[128,512]{1,0:T(8,128)(2,1)}, bf16[128,512]{1,0:T(8,128)(2,1)}, bf16[128,512]{1,0:T(8,128)(2,1)}, bf16[5...) custom-call(bf16[128,512]{1,0:T(8,128)(2,1)} %sq_in.1, bf16[128,512]{1,0:T(8,128)(2,1)} %sk.1, bf16[128,512]{1,0:T(8,128)(2,1)} %sv.1, ...), custom_call_target="tpu_custom_call" | custom-call | tf_op jit(solution)/shard_map/pallas_call | solution.py:602
  39.0 17.1 %shard_map.163 = (bf16[128,512]{1,0:T(8,128)(2,1)}, bf16[128,512]{1,0:T(8,128)(2,1)}, bf16[128,512]{1,0:T(8,128)(2,1)}, bf16[128,512]{1,0:T(8,128)(2,1)}, bf16[1...) custom-call(bf16[128,512]{1,0:T(8,128)(2,1)} %get-tuple-element.13.sq_done, ...), custom_call_target="tpu_custom_call" | custom-call | tf_op jit(solution)/shard_map/pallas_call | solution.py:654
where the time goes:
time: 56.2 us; the launch traced here: 56.1 us
  Pallas kernels  55.4 us (99%)
  between operations  0.64 us (1%)
    pallas_call x1, Pallas kernels, dense_body(): pl.pallas_call(functools.partial(operator_kernel, n, m), out_shape=[token...  38.3 us
    pallas_call x1, Pallas kernels, dense_body(): pl.pallas_call(finish_kernel, out_shape=[tokens] * 3 + [short] + [tokens]...  17.1 us

commit v1 on v0

--- a/solution.py
+++ b/solution.py
@@ -285,18 +285,22 @@
     loads["og"].wait()
     pl.semaphore_wait(barrier, n + m - 2)
 
-    og_copies = []
-    for d in range(1, m):
+    col_pair = col + 1 - 2 * lax.rem(col, 2)
+
+    def og_copy(slot, source, peer):
         copy = pltpu.make_async_remote_copy(
-            src_ref=og,
-            dst_ref=og_rx.at[d - 1],
-            send_sem=og_send.at[d - 1],
-            recv_sem=og_recv.at[d - 1],
-            device_id=(me, lax.rem(col + d, m)),
+            src_ref=source,
+            dst_ref=og_rx.at[slot],
+            send_sem=og_send.at[slot],
+            recv_sem=og_recv.at[slot],
+            device_id=(me, peer),
             device_id_type=MESH,
         )
         copy.start()
-        og_copies.append(copy)
+        return copy
+
+    og_far = [og_copy(d, og, lax.rem(col + 2 * d, m)) for d in range(1, m // 2)]
+    og_near = [og_copy(0, og, col_pair)]
 
     own_rows = pl.ds(pl.multiple_of(me * cb, cb), cb)
     sent = {}
@@ -353,6 +357,10 @@
         cos_at, sin_at = tiles(k)
         return dot(rows_in, fwd[:depth, cos_at]), dot(rows_in, fwd[:depth, sin_at])
 
+    for d in range(1, m // 2):
+        og_far[d - 1].wait_recv()
+        og_near.append(og_copy(m // 2 - 1 + d, og_rx.at[d], col_pair))
+
     arrived("prod")
     for s in range(n):
         signals[0:cb, s * rows : (s + 1) * rows] = rx_prod[s]
@@ -370,7 +378,7 @@
         waves[0:cb, sin_at] = (pc * fs + ps * fc).astype(BF16)
         return carry
 
-    lax.fori_loop(0, seq // kt, short_step, 0)
+    lax.fori_loop(0, seq // kt, short_step, 0, unroll=True)
     loads["inv"].wait()
 
     def at_tokens(step):
@@ -386,20 +394,23 @@
         put(tx_smix, step, mix)
         return carry
 
-    lax.fori_loop(0, n // 2, short_back, 0)
+    lax.fori_loop(0, n // 2, short_back, 0, unroll=True)
 
     loads["weight"].wait()
     loads["lq"].wait()
-    total = jnp.zeros((chans, rows), F32)
-    for d in range(m):
-        if d > 0:
-            og_copies[d - 1].wait_recv()
-        owner = lax.rem(col + m - d, m)
+    def projected(owner, block):
         features = pl.ds(pl.multiple_of(owner * chans, chans), chans)
-        block = og[...] if d == 0 else og_rx[d - 1]
-        total = total + lax.dot_general(
+        return lax.dot_general(
             weight_v[:, features], block, (((1,), (1,)), ((), ())), preferred_element_type=F32
         )
+
+    total = projected(col, og[...])
+    for d in range(1, m // 2):
+        total = total + projected(lax.rem(col + m - 2 * d, m), og_rx[d])
+    for place, copy in enumerate(og_near):
+        copy.wait_recv()
+        owner = lax.rem(col_pair + m - 2 * place, m)
+        total = total + projected(owner, og_rx[0 if place == 0 else m // 2 - 1 + place])
     grad[...] = total.astype(BF16)
     tx_grad[...] = (grad[...].astype(F32) * lq[...].astype(F32).T).astype(BF16)
     exchange("grad", lambda peer: tx_grad.at[row_block(peer)], rx_grad.at[me])
@@ -424,13 +435,13 @@
         waves[0:cb, sin_at] = (c[0:cb] * s[cb:] + s[0:cb] * c[cb:]).astype(BF16)
         return carry
 
-    lax.fori_loop(0, seq // kt, long_step, 0)
+    lax.fori_loop(0, seq // kt, long_step, 0, unroll=True)
 
     def mix_back(step, carry):
         put(tx_lmix, step, dot(waves[0:cb, :], inv[:, at_tokens(step)]) * (1.0 / seq))
         return carry
 
-    lax.fori_loop(0, n // 2, mix_back, 0)
+    lax.fori_loop(0, n // 2, mix_back, 0, unroll=True)
     exchange("lmix", lambda peer: tx_lmix.at[peer], lmix_rx.at[own_rows])
     lmix_rx[own_rows, :] = tx_lmix[me]
 
@@ -449,7 +460,7 @@
         waves[2 * cb : 3 * cb, sin_at] = (uc * s - us * c).astype(BF16)
         return carry
 
-    lax.fori_loop(0, seq // kt, grad_step, 0)
+    lax.fori_loop(0, seq // kt, grad_step, 0, unroll=True)
 
     def long_back(step, carry):
         mixes = dot(waves[cb:, :], inv[:, at_tokens(step)]) * (1.0 / seq)
@@ -458,7 +469,7 @@
         smix[:, at_tokens(step)] = mixes[0:cb]
         return carry
 
-    lax.fori_loop(0, n // 2, long_back, 0)
+    lax.fori_loop(0, n // 2, long_back, 0, unroll=True)
     for part, source, target in (
         ("back", tx_back, back_rx), ("filt", tx_filt, filt_rx)
     ):
@@ -480,7 +491,7 @@
         waves[cb : 2 * cb, sin_at] = (pc * s - ps * c).astype(BF16)
         return carry
 
-    lax.fori_loop(0, seq // kt, gate_step, 0)
+    lax.fori_loop(0, seq // kt, gate_step, 0, unroll=True)
 
     terms = dot(waves[cb : 2 * cb, :], inv[:, 0:taps]) * (1.0 / (seq * math.sqrt(seq)))
     tx_taps[...] = terms.astype(BF16)
@@ -508,7 +519,7 @@
         put(tx_bone, step, dot(waves[0:cb, :], inv[:, at_tokens(step)]) * (1.0 / seq))
         return carry
 
-    lax.fori_loop(0, n // 2, short_grad, 0)
+    lax.fori_loop(0, n // 2, short_grad, 0, unroll=True)
     exchange("bone", lambda peer: tx_bone.at[peer], bone_out.at[own_rows])
     keep(tx_bone.at[me], bone_out.at[own_rows])
 
@@ -543,7 +554,7 @@
     for part in PARTS:
         for copy in sent[part]:
             copy.wait_send()
-    for copy in og_copies + far + near:
+    for copy in og_far + og_near + far + near:
         copy.wait_send()
     for copy in kept:
         copy.wait()
@@ -552,7 +563,7 @@
 def finish_kernel(
     sq_done, lq_done, lk_done, lf_done, bone, taps, sk, sv,
     sq_grad, sk_grad, sv_grad, sf_grad, lq_grad, lk_grad, lf_grad,
-    bone_v, taps_v, sk_v, sv_v, sk_out, sv_out, sf_out, move_sem,
+    bone_v, taps_v, sk_v, sv_v, sk_out, sv_out, sf_out, done_v, move_sem,
 ):
     def move(place, source, target):
         copy = pltpu.make_async_copy(source, target, move_sem.at[place])
@@ -565,12 +576,14 @@
             ((bone, bone_v), (sv, sv_v), (sk, sk_v), (taps, taps_v))
         )
     ]
-    moves = [
-        move(4 + place, source, target)
-        for place, (source, target) in enumerate(
-            ((sq_done, sq_grad), (lq_done, lq_grad), (lk_done, lk_grad), (lf_done, lf_grad))
-        )
+    done = [
+        move(4 + place, source, done_v.at[place])
+        for place, source in enumerate((sq_done, lq_done, lk_done, lf_done))
     ]
+    moves = []
+    for place, target in enumerate((sq_grad, lq_grad, lk_grad, lf_grad)):
+        done[place].wait()
+        moves.append(move(11 + place, done_v.at[place], target))
     loads[0].wait()
     back_one = bone_v[...].astype(F32).T
     loads[1].wait()
@@ -664,7 +677,8 @@
             pltpu.VMEM((rows, chans), BF16),
             pltpu.VMEM((rows, chans), BF16),
             pltpu.VMEM((taps, chans), BF16),
-            pltpu.SemaphoreType.DMA((11,)),
+            pltpu.VMEM((4, rows, chans), BF16),
+            pltpu.SemaphoreType.DMA((15,)),
         ],
         compiler_params=pltpu.CompilerParams(vmem_limit_bytes=VMEM_GRANT),
     )(*sent_on, sk, sv)
@@ -681,6 +695,7 @@
         and n > 1
         and n % 2 == 0
         and m > 1
+        and m % 2 == 0
         and chans % (16 * n) == 0
         and chans % 128 == 0
     )

time: 56.2 us -> 40.4 us (0.72)
  Pallas kernels: 55.4 us -> 39.6 us
    pallas_call x1, Pallas kernels: 17.1 us -> 2.35 us  [dense_body(): pl.pallas_call(finish_kernel, out_shape=[tokens] * 3 + [short] + [tokens]...]
    pallas_call x1, Pallas kernels: 38.3 us -> 37.2 us  [dense_body(): pl.pallas_call(functools.partial(operator_kernel, n, m), out_shape=[token...]
where the time goes in v1:
time: 40.4 us; the launch traced here: 40.2 us
  Pallas kernels  39.6 us (98%)
  between operations  0.64 us (2%)
    pallas_call x1, Pallas kernels, dense_body(): pl.pallas_call(functools.partial(operator_kernel, n, m), out_shape=[token...  37.2 us
    pallas_call x1, Pallas kernels, dense_body(): pl.pallas_call(finish_kernel, out_shape=[tokens] * 3 + [short] + [tokens]...  2.35 us

profile of v1, /device:TPU:0, one launch (start us, length us, event | category | flops | bytes accessed | tf_op | source)
XLA Modules:
  0.0 40.2 jit_solution(4737511773131631151)
XLA Ops:
  0.6 37.2 %shard_map.162 = (bf16[128,512]{1,0:T(8,128)(2,1)}, bf16[128,512]{1,0:T(8,128)(2,1)}, bf16[128,512]{1,0:T(8,128)(2,1)}, bf16[128,512]{1,0:T(8,128)(2,1)}, bf16[5...) custom-call(bf16[128,512]{1,0:T(8,128)(2,1)} %sq_in.1, bf16[128,512]{1,0:T(8,128)(2,1)} %sk.1, bf16[128,512]{1,0:T(8,128)(2,1)} %sv.1, ...), custom_call_target="tpu_custom_call" | custom-call | tf_op jit(solution)/shard_map/pallas_call | solution.py:615
  37.9 2.3 %shard_map.163 = (bf16[128,512]{1,0:T(8,128)(2,1)}, bf16[128,512]{1,0:T(8,128)(2,1)}, bf16[128,512]{1,0:T(8,128)(2,1)}, bf16[128,512]{1,0:T(8,128)(2,1)}, bf16[1...) custom-call(bf16[128,512]{1,0:T(8,128)(2,1)} %get-tuple-element.13.sq_done, ...), custom_call_target="tpu_custom_call" | custom-call | tf_op jit(solution)/shard_map/pallas_call | solution.py:667

commit v2 on v1

--- a/solution.py
+++ b/solution.py
@@ -238,6 +238,20 @@
     return jnp.dot(a, b, preferred_element_type=F32)
 
 
+def partner(index, step, size):
+    bit = 1
+    while bit < size:
+        if step & bit:
+            index = index + bit - 2 * bit * lax.rem(lax.div(index, bit), 2)
+        bit *= 2
+    return index
+
+
+def steps_of(size):
+    far, near = list(range(size // 2, size)), list(range(1, size // 2))
+    return [step for pair in zip(far, near + [0]) for step in pair if step > 0]
+
+
 def flipped(block):
     return block.astype(F32).T.astype(BF16)
 
@@ -308,8 +322,8 @@
     def exchange(part, source, target):
         place = PARTS.index(part)
         copies = []
-        for d in range(1, n):
-            peer = lax.rem(me + d, n)
+        for d in steps_of(n):
+            peer = partner(me, d, n)
             copy = pltpu.make_async_remote_copy(
                 src_ref=source(peer),
                 dst_ref=target,
@@ -511,7 +525,8 @@
         return copy
 
     far = [
-        taps_copy(d - 1, tx_taps, own_rows, lax.rem(me + 2 * d, n)) for d in range(1, n // 2)
+        taps_copy(d - 1, tx_taps, own_rows, partner(me, 2 * d, n))
+        for d in range(n // 2 - 1, 0, -1)
     ]
     near = [taps_copy(n // 2 - 1, tx_taps, own_rows, pair)]
 
@@ -543,8 +558,8 @@
     finish(3, lf_grad, filt_rx[...].astype(F32))
 
     for d in range(1, n // 2):
-        far[d - 1].wait_recv()
-        source = row_block(lax.rem(me + n - 2 * d, n))
+        far[n // 2 - 1 - d].wait_recv()
+        source = row_block(partner(me, 2 * d, n))
         near.append(taps_copy(n // 2 - 1 + d, taps_rx.at[source], source, pair))
     for copy in near:
         copy.wait_recv()
@@ -693,7 +708,7 @@
         and taps % 128 == 0
         and taps <= rows * n
         and n > 1
-        and n % 2 == 0
+        and n & (n - 1) == 0
         and m > 1
         and m % 2 == 0
         and chans % (16 * n) == 0

time: 40.4 us -> 41.2 us (1.020)
  Pallas kernels: 39.6 us -> 40.5 us
    pallas_call x1, Pallas kernels: 37.2 us -> 38.1 us  [dense_body(): pl.pallas_call(functools.partial(operator_kernel, n, m), out_shape=[token...]
where the time goes in v2:
time: 41.2 us; the launch traced here: 41.1 us
  Pallas kernels  40.5 us (98%)
  between operations  0.64 us (2%)
    pallas_call x1, Pallas kernels, dense_body(): pl.pallas_call(functools.partial(operator_kernel, n, m), out_shape=[token...  38.1 us
    pallas_call x1, Pallas kernels, dense_body(): pl.pallas_call(finish_kernel, out_shape=[tokens] * 3 + [short] + [tokens]...  2.35 us

profile of v2, /device:TPU:0, one launch (start us, length us, event | category | flops | bytes accessed | tf_op | source)
XLA Modules:
  0.0 41.1 jit_solution(16137967620932136439)
XLA Ops:
  0.6 38.1 %shard_map.162 = (bf16[128,512]{1,0:T(8,128)(2,1)}, bf16[128,512]{1,0:T(8,128)(2,1)}, bf16[128,512]{1,0:T(8,128)(2,1)}, bf16[128,512]{1,0:T(8,128)(2,1)}, bf16[5...) custom-call(bf16[128,512]{1,0:T(8,128)(2,1)} %sq_in.1, bf16[128,512]{1,0:T(8,128)(2,1)} %sk.1, bf16[128,512]{1,0:T(8,128)(2,1)} %sv.1, ...), custom_call_target="tpu_custom_call" | custom-call | tf_op jit(solution)/shard_map/pallas_call | solution.py:630
  38.7 2.3 %shard_map.163 = (bf16[128,512]{1,0:T(8,128)(2,1)}, bf16[128,512]{1,0:T(8,128)(2,1)}, bf16[128,512]{1,0:T(8,128)(2,1)}, bf16[128,512]{1,0:T(8,128)(2,1)}, bf16[1...) custom-call(bf16[128,512]{1,0:T(8,128)(2,1)} %get-tuple-element.13.sq_done, ...), custom_call_target="tpu_custom_call" | custom-call | tf_op jit(solution)/shard_map/pallas_call | solution.py:682

commit v3 on v1

--- a/solution.py
+++ b/solution.py
@@ -530,6 +530,10 @@
     arrived("smix")
     arrived("lmix")
     finish(0, lq_grad, grad[...].astype(F32) * lmix_rx[...].astype(F32))
+    for d in range(1, n // 2):
+        far[d - 1].wait_recv()
+        source = row_block(lax.rem(me + n - 2 * d, n))
+        near.append(taps_copy(n // 2 - 1 + d, taps_rx.at[source], source, pair))
     arrived("back")
     back = back_rx[...].astype(F32).T
     mix = smix_rx[...].astype(F32).T
@@ -542,10 +546,6 @@
     arrived("filt")
     finish(3, lf_grad, filt_rx[...].astype(F32))
 
-    for d in range(1, n // 2):
-        far[d - 1].wait_recv()
-        source = row_block(lax.rem(me + n - 2 * d, n))
-        near.append(taps_copy(n // 2 - 1 + d, taps_rx.at[source], source, pair))
     for copy in near:
         copy.wait_recv()
     keep(taps_rx, taps_out)

time: 40.4 us -> 39.9 us (0.988)
  Pallas kernels: 39.6 us -> 39.1 us
    pallas_call x1, Pallas kernels: 37.2 us -> 36.8 us  [dense_body(): pl.pallas_call(functools.partial(operator_kernel, n, m), out_shape=[token...]
where the time goes in v3:
time: 39.9 us; the launch traced here: 39.8 us
  Pallas kernels  39.1 us (98%)
  between operations  0.64 us (2%)
    pallas_call x1, Pallas kernels, dense_body(): pl.pallas_call(functools.partial(operator_kernel, n, m), out_shape=[token...  36.8 us
    pallas_call x1, Pallas kernels, dense_body(): pl.pallas_call(finish_kernel, out_shape=[tokens] * 3 + [short] + [tokens]...  2.35 us

profile of v3, /device:TPU:0, one launch (start us, length us, event | category | flops | bytes accessed | tf_op | source)
XLA Modules:
  0.0 39.8 jit_solution(6094395325225213523)
XLA Ops:
  0.6 36.8 %shard_map.162 = (bf16[128,512]{1,0:T(8,128)(2,1)}, bf16[128,512]{1,0:T(8,128)(2,1)}, bf16[128,512]{1,0:T(8,128)(2,1)}, bf16[128,512]{1,0:T(8,128)(2,1)}, bf16[5...) custom-call(bf16[128,512]{1,0:T(8,128)(2,1)} %sq_in.1, bf16[128,512]{1,0:T(8,128)(2,1)} %sk.1, bf16[128,512]{1,0:T(8,128)(2,1)} %sv.1, ...), custom_call_target="tpu_custom_call" | custom-call | tf_op jit(solution)/shard_map/pallas_call | solution.py:615
  37.4 2.3 %shard_map.163 = (bf16[128,512]{1,0:T(8,128)(2,1)}, bf16[128,512]{1,0:T(8,128)(2,1)}, bf16[128,512]{1,0:T(8,128)(2,1)}, bf16[128,512]{1,0:T(8,128)(2,1)}, bf16[1...) custom-call(bf16[128,512]{1,0:T(8,128)(2,1)} %get-tuple-element.13.sq_done, ...), custom_call_target="tpu_custom_call" | custom-call | tf_op jit(solution)/shard_map/pallas_call | solution.py:667
